TPU v7x, 768 devices: a whole 4x8x12 slice. The times are simulated.
768 devices in a mesh: dp: 12 (over z), pool: 64 (over y, x, core).
Axes of the slice: x: 4, y: 8, z: 12, core: 2. Of those that a mesh axis runs over, the one named last changes fastest.
Arguments:
- queries: bfloat16 [1572864, 128], P(('dp', 'pool')), may hold values from -6 to 6
- cotangent: bfloat16 [1572864, 128], P(('dp', 'pool')), may hold values from -6 to 6
- owner: int32 [24576, 1], P(('dp', 'pool')), may hold values from 0 to 63; in each aligned block of 32 rows (0 to 31, 32 to 63, ...) at most 2 rows name the same one
- row: int32 [24576], P(('dp', 'pool')), may hold values from 0 to 7
- table: bfloat16 [6144, 256, 256], P(('dp', 'pool')), may hold values from -6 to 6
- lengths: int32 [6144, 2], P(('dp', 'pool')), may hold values from 16 to 128
- bias: float32 [1, 256], replicated, may hold values from -4 to 4
Outputs:
- attended: bfloat16 [1572864, 128], P(('dp', 'pool'))
- query_gradient: bfloat16 [1572864, 128], P(('dp', 'pool'))
- table_grad: bfloat16 [6144, 256, 256], P(('dp', 'pool'))
- bias_grad: float32 [1, 256], replicated
Inputs may be any that keep to these rules, and one draw needn't show every extreme that they name: Among the spans of one device at most 2 name the same owner; some owner is named by exactly 2 of them on some devices.
All inputs are finite; a program needn't handle non-finite values.
Results may differ from a plain program's by a relative error of at most 0.0067.
Values may be sent and summed in bfloat16 or wider, within the bound.
A program may use at most 128 MiB of HBM per device.

v0:
```python
import jax
import jax.numpy as jnp
from jax import lax
from jax.sharding import PartitionSpec as P

NEIGH = 2


def block_scores(query_block, kv_blk, len_blk, row_bias_values, nbr_len):
    width = query_block.shape[-1]
    neighbour_keys = kv_blk[:, :, :width]
    position = jnp.arange(kv_blk.shape[1], dtype=jnp.int32)
    limit = jnp.repeat(len_blk, nbr_len, axis=1)
    live = (position % nbr_len)[None, :] < limit
    attention_scores = (
        jnp.einsum("sqd,skd->sqk", query_block, neighbour_keys, preferred_element_type=jnp.float32)
        * width ** (-0.5)
        + row_bias_values[None, None, :]
    )
    return jnp.where(live[:, None, :], attention_scores, -1e30)


def block_forward(query_block, kv_blk, len_blk, row_bias_values, nbr_len):
    width = query_block.shape[-1]
    attention_scores = block_scores(query_block, kv_blk, len_blk, row_bias_values, nbr_len)
    peak = jnp.max(attention_scores, axis=-1, keepdims=True)
    lse = peak + jnp.log(jnp.sum(jnp.exp(attention_scores - peak), axis=-1, keepdims=True))
    probs = jnp.exp(attention_scores - lse)
    attention_weights = probs.astype(jnp.bfloat16)
    attended = jnp.einsum(
        "sqk,skd->sqd", attention_weights, kv_blk[:, :, width:], preferred_element_type=jnp.float32
    ).astype(jnp.bfloat16)
    return (probs, attention_weights, attended, lse)


def block_backward(
    query_block,
    kv_blk,
    probs,
    attention_weights,
    incoming_cotangent_block,
    delta,
    picked_blk,
    used_blk,
    nsets,
):
    width = query_block.shape[-1]
    score_scale = width ** (-0.5)
    weight_gradient = jnp.einsum(
        "sqd,skd->sqk",
        incoming_cotangent_block,
        kv_blk[:, :, width:],
        preferred_element_type=jnp.float32,
    )
    dscores = probs * (weight_gradient - delta)
    bias_part = jnp.sum(dscores, axis=(0, 1))
    scaled_score_gradient = (dscores * score_scale).astype(jnp.bfloat16)
    query_gradient = jnp.einsum(
        "sqk,skd->sqd",
        scaled_score_gradient,
        kv_blk[:, :, :width],
        preferred_element_type=jnp.float32,
    ).astype(jnp.bfloat16)
    key_gradient = jnp.einsum(
        "sqk,sqd->skd", scaled_score_gradient, query_block, preferred_element_type=jnp.float32
    )
    value_gradient = jnp.einsum(
        "sqk,sqd->skd",
        attention_weights,
        incoming_cotangent_block,
        preferred_element_type=jnp.float32,
    )
    kv_grad = jnp.concatenate([key_gradient, value_gradient], axis=-1)
    selector = (
        (picked_blk[:, None] == jnp.arange(nsets, dtype=jnp.int32)[None, :]) & used_blk[:, None]
    ).astype(jnp.float32)
    grad_part = jnp.einsum("sn,skd->nkd", selector, kv_grad, precision=lax.Precision.HIGHEST)
    return (grad_part, bias_part, query_gradient)


def body(queries, cotangent, owner, row, table, lengths, bias):
    npool = lax.axis_size("pool")
    nchunks = owner.shape[0]
    width = queries.shape[1]
    span = queries.shape[0] // nchunks
    keys_all = table.shape[1]
    nbr_len = keys_all // NEIGH
    nsets = table.shape[0]
    capacity = max(2, 2 * nchunks // npool)
    slots = npool * capacity
    group = 16
    nblocks = slots // group
    row_bias_values = bias.reshape(keys_all)
    target = owner[:, 0]
    hits = (target[:, None] == jnp.arange(npool, dtype=jnp.int32)[None, :]).astype(jnp.int32)
    before = jnp.cumsum(hits, axis=0) - hits
    rank = jnp.sum(before * hits, axis=1)
    slot_id = target * capacity + rank
    query_spans = queries.reshape(nchunks, span, width)
    query_send = jnp.zeros((slots, span, width), jnp.bfloat16).at[slot_id].set(query_spans)
    row_send = jnp.full((slots,), -1, jnp.int32).at[slot_id].set(row)
    query_recv, row_recv = (
        lax.all_to_all(
            query_send.reshape(npool, capacity, span, width),
            "pool",
            split_axis=0,
            concat_axis=0,
            tiled=True,
        ),
        lax.all_to_all(
            row_send.reshape(npool, capacity), "pool", split_axis=0, concat_axis=0, tiled=True
        ),
    )
    query_recv = query_recv.reshape(nblocks, group, span, width)
    row_recv = row_recv.reshape(nblocks, group)
    picked = jnp.maximum(row_recv, 0)
    used = row_recv >= 0
    cot_spans = cotangent.reshape(nchunks, span, width)
    cot_send = (
        jnp.zeros((slots, span, width), jnp.bfloat16)
        .at[slot_id]
        .set(cot_spans)
        .reshape(npool, capacity, span, width)
    )
    start = (
        jnp.zeros((nsets, keys_all, 2 * width), jnp.float32),
        jnp.zeros((keys_all,), jnp.float32),
    )

    def forward_block(carry, pieces):
        query_block, picked_blk = pieces
        kv_blk = table[picked_blk]
        probs, attention_weights, attended_blk, lse = block_forward(
            query_block, kv_blk, lengths[picked_blk], row_bias_values, nbr_len
        )
        return (carry, (attended_blk, lse))

    _, (owner_out, owner_lse) = lax.scan(forward_block, 0, (query_recv, picked))
    answer = lax.all_to_all(
        owner_out.reshape(npool, capacity, span, width),
        "pool",
        split_axis=0,
        concat_axis=0,
        tiled=True,
    )
    cot_recv = lax.all_to_all(cot_send, "pool", split_axis=0, concat_axis=0, tiled=True)
    cot_recv = cot_recv.reshape(nblocks, group, span, width)
    delta_recv = jnp.sum(
        cot_recv.astype(jnp.float32) * owner_out.astype(jnp.float32), axis=-1, keepdims=True
    )

    def backward_block(carry, pieces):
        grad_acc, bias_acc = carry
        query_block, picked_blk, used_blk, lse, incoming_cotangent_block, delta = pieces
        kv_blk = table[picked_blk]
        attention_scores = block_scores(
            query_block, kv_blk, lengths[picked_blk], row_bias_values, nbr_len
        )
        probs = jnp.exp(attention_scores - lse)
        attention_weights = probs.astype(jnp.bfloat16)
        grad_part, bias_part, query_gradient = block_backward(
            query_block,
            kv_blk,
            probs,
            attention_weights,
            incoming_cotangent_block,
            delta,
            picked_blk,
            used_blk,
            nsets,
        )
        return ((grad_acc + grad_part, bias_acc + bias_part), query_gradient)

    (grad_acc, bias_acc), owner_qgrad = lax.scan(
        backward_block, start, (query_recv, picked, used, owner_lse, cot_recv, delta_recv)
    )
    attended = answer.reshape(slots, span, width)[slot_id].reshape(nchunks * span, width)
    returned = lax.all_to_all(
        owner_qgrad.reshape(npool, capacity, span, width),
        "pool",
        split_axis=0,
        concat_axis=0,
        tiled=True,
    )
    query_gradient = returned.reshape(slots, span, width)[slot_id].reshape(nchunks * span, width)
    bias_local = bias_acc.reshape(bias.shape)
    bias_grad = lax.psum(bias_local, ("dp", "pool"))
    return (attended, query_gradient, grad_acc.astype(jnp.bfloat16), bias_grad)


def solution(mesh):
    return jax.shard_map(
        body,
        mesh=mesh,
        in_specs=(
            P(("dp", "pool"), None),
            P(("dp", "pool"), None),
            P(("dp", "pool"), None),
            P(("dp", "pool")),
            P(("dp", "pool"), None, None),
            P(("dp", "pool"), None),
            P(),
        ),
        out_specs=(
            P(("dp", "pool"), None),
            P(("dp", "pool"), None),
            P(("dp", "pool"), None, None),
            P(),
        ),
        check_vma=False,
    )
```

profile of v0, /device:TPU:1, one launch (start us, length us, event | category | flops | bytes accessed | tf_op | source)
XLA Modules:
  0.0 502.4 jit_solution(9505514027286289358)
XLA Ops:
  4.5 14.5 %all-to-all-start = ((s32[64,1,2]{2,1,0:T(1,128)}), s32[64,1,2]{2,1,0:T(1,128)S(1)}, u32[]{:S(2)}, u32[]{:S(2)}) async-start(s32[64,1,2]{2,1,0:T(1,128)} %bitcast.9), calls=%async_computation | async-start | bytes 65536 | tf_op jit(solution)/shard_map/all_to_all | solution.py:110
  28.5 7.5 %all-to-all-start.1 = ((bf16[64,2,64,128]{3,2,1,0:T(8,128)(2,1)}), bf16[64,2,64,128]{3,2,1,0:T(8,128)(2,1)}, u32[]{:S(2)}, u32[]{:S(2)}) async-start(bf16[64,2,64,128]{3,2,1,0:T(8,128)(2,1)} %bitcast.11), calls=%async_computation.1 | async-start | bytes 4194304 | tf_op jit(solution)/shard_map/all_to_all | solution.py:103
  42.8 42.8 %all-to-all-done.1 = bf16[64,2,64,128]{3,2,1,0:T(8,128)(2,1)} async-done(((bf16[64,2,64,128]{3,2,1,0:T(8,128)(2,1)}), bf16[64,2,64,128]{3,2,1,0:T(8,128)(2,1)}, u32[]{:S(2)}, u32[]{:S(2)}) %all-to-all-start.1) | async-done | bytes 2097184 | tf_op jit(solution)/shard_map/all_to_all | solution.py:103
  85.6 7.2 %all-to-all-start.3 = ((bf16[64,2,64,128]{3,2,1,0:T(8,128)(2,1)}), bf16[64,2,64,128]{3,2,1,0:T(8,128)(2,1)}, u32[]{:S(2)}, u32[]{:S(2)}) async-start(bf16[64,2,64,128]{3,2,1,0:T(8,128)(2,1)} %bitcast.17), calls=%async_computation.3 | async-start | bytes 4194304 | tf_op jit(solution)/shard_map/all_to_all | solution.py:146
  94.7 35.3 %while.31 = (s32[]{:T(128)}, bf16[8,16,64,128]{3,2,1,0:T(8,128)(2,1)}, f32[8,16,64,1]{2,1,3,0:T(8,128)S(1)}, s32[8,16]{1,0:T(8,128)S(1)}, s32[8,2]{1,0:T(8,128)S...) while((s32[]{:T(128)}, ...), condition=%wide.region_7.8_spmd, body=%wide.region_4.0_spmd.sunk | while | flops 136451632 | bytes 10063669 | solution.py:138
  130.0 12.4 %all-to-all-done.3 = bf16[64,2,64,128]{3,2,1,0:T(8,128)(2,1)} async-done(((bf16[64,2,64,128]{3,2,1,0:T(8,128)(2,1)}), bf16[64,2,64,128]{3,2,1,0:T(8,128)(2,1)}, u32[]{:S(2)}, u32[]{:S(2)}) %all-to-all-start.3) | async-done | bytes 2097184 | tf_op jit(solution)/shard_map/all_to_all | solution.py:146
  142.4 7.4 %all-to-all-start.2 = ((bf16[64,2,64,128]{3,2,1,0:T(8,128)(2,1)}), bf16[64,2,64,128]{3,2,1,0:T(8,128)(2,1)}, u32[]{:S(2)}, u32[]{:S(2)}) async-start(bf16[64,2,64,128]{3,2,1,0:T(8,128)(2,1)} %bitcast.132), calls=%async_computation.2 | async-start | bytes 4194304 | tf_op jit(solution)/shard_map/all_to_all | solution.py:139
  154.7 179.6 %while.32 = (s32[]{:T(128)}, f32[8,256,256]{2,0,1:T(8,128)}, f32[256]{0:T(256)S(1)}, bf16[8,16,64,128]{3,2,1,0:T(8,128)(2,1)}, s32[8,16]{1,0:T(8,128)S(1)}, /*in...) while((s32[]{:T(128)}, f32[8,256,256]{2,0,1:T(8,128)}, ...), condition=%wide.region_12.13_spmd.clone, body=%wide.region_10.12_spmd.clone.sunk | while | flops 441588800 | bytes 61165736 | solution.py:174
  165.2 5.6 %copy.33 = f32[16,256,256]{2,0,1:T(8,128)} copy(f32[16,256,256]{1,2,0:T(8,128)} %pad_maximum_fusion.2) | data formatting | bytes 8388608 | tf_op jit(solution)/shard_map/while/body/eval_jaxpr/concatenate | solution.py:73
  170.9 4.9 select_add_fusion.4
  187.7 5.6 %copy.33 = f32[16,256,256]{2,0,1:T(8,128)} copy(f32[16,256,256]{1,2,0:T(8,128)} %pad_maximum_fusion.2) | data formatting | bytes 8388608 | tf_op jit(solution)/shard_map/while/body/eval_jaxpr/concatenate | solution.py:73
  193.3 4.9 select_add_fusion.4
  210.1 5.6 %copy.33 = f32[16,256,256]{2,0,1:T(8,128)} copy(f32[16,256,256]{1,2,0:T(8,128)} %pad_maximum_fusion.2) | data formatting | bytes 8388608 | tf_op jit(solution)/shard_map/while/body/eval_jaxpr/concatenate | solution.py:73
  215.8 4.9 select_add_fusion.4
  232.6 5.6 %copy.33 = f32[16,256,256]{2,0,1:T(8,128)} copy(f32[16,256,256]{1,2,0:T(8,128)} %pad_maximum_fusion.2) | data formatting | bytes 8388608 | tf_op jit(solution)/shard_map/while/body/eval_jaxpr/concatenate | solution.py:73
  238.2 4.9 select_add_fusion.4
  255.0 5.6 %copy.33 = f32[16,256,256]{2,0,1:T(8,128)} copy(f32[16,256,256]{1,2,0:T(8,128)} %pad_maximum_fusion.2) | data formatting | bytes 8388608 | tf_op jit(solution)/shard_map/while/body/eval_jaxpr/concatenate | solution.py:73
  260.7 4.9 select_add_fusion.4
  277.5 5.6 %copy.33 = f32[16,256,256]{2,0,1:T(8,128)} copy(f32[16,256,256]{1,2,0:T(8,128)} %pad_maximum_fusion.2) | data formatting | bytes 8388608 | tf_op jit(solution)/shard_map/while/body/eval_jaxpr/concatenate | solution.py:73
  300.0 5.6 %copy.33 = f32[16,256,256]{2,0,1:T(8,128)} copy(f32[16,256,256]{1,2,0:T(8,128)} %pad_maximum_fusion.2) | data formatting | bytes 8388608 | tf_op jit(solution)/shard_map/while/body/eval_jaxpr/concatenate | solution.py:73
  305.6 4.9 select_add_fusion.4
  322.4 5.6 %copy.33 = f32[16,256,256]{2,0,1:T(8,128)} copy(f32[16,256,256]{1,2,0:T(8,128)} %pad_maximum_fusion.2) | data formatting | bytes 8388608 | tf_op jit(solution)/shard_map/while/body/eval_jaxpr/concatenate | solution.py:73
  334.3 10.6 %all-to-all-start.4 = ((bf16[64,2,64,128]{3,2,1,0:T(8,128)(2,1)}), bf16[64,2,64,128]{3,2,1,0:T(8,128)(2,1)}, u32[]{:S(2)}, u32[]{:S(2)}) async-start(bf16[64,2,64,128]{3,2,1,0:T(8,128)(2,1)} %bitcast.133), calls=%async_computation.4 | async-start | bytes 4194304 | tf_op jit(solution)/shard_map/all_to_all | solution.py:178
  346.5 149.9 %psum.7 = f32[1,256]{1,0:T(1,128)} all-reduce(f32[1,256]{1,0:T(1,128)S(1)} %bitcast.141), channel_id=1, replica_groups=mesh['dp'=12,'pool'=64] {'dp','pool'}, use_global_device_ids=true, to_apply=%region_13.14 | all-reduce | flops 256 | bytes 2048 | tf_op jit(solution)/shard_map/psum | solution.py:187
  (300 shorter events, 173.5 us)
Async XLA Ops:
  0.6 20.3 %copy-start.5 = (bf16[2048,128]{1,0:T(8,128)(2,1)S(1)}, bf16[2048,128]{1,0:T(8,128)(2,1)}, u32[]{:S(2)}) copy-start(bf16[2048,128]{1,0:T(8,128)(2,1)} %param.11) | copy-start | bytes 1572868
  4.5 24.0 %all-to-all-start = ((s32[64,1,2]{2,1,0:T(1,128)}), s32[64,1,2]{2,1,0:T(1,128)S(1)}, u32[]{:S(2)}, u32[]{:S(2)}) async-start(s32[64,1,2]{2,1,0:T(1,128)} %bitcast.9), calls=%async_computation | async-start | bytes 65536 | tf_op jit(solution)/shard_map/all_to_all | solution.py:110
  28.5 7.6 %copy-start.7 = (s32[8,2]{0,1:T(2,128)S(1)}, s32[8,2]{0,1:T(2,128)}, u32[]{:S(2)}) copy-start(s32[8,2]{0,1:T(2,128)} %param.16) | copy-start | bytes 196
  28.5 57.1 %all-to-all-start.1 = ((bf16[64,2,64,128]{3,2,1,0:T(8,128)(2,1)}), bf16[64,2,64,128]{3,2,1,0:T(8,128)(2,1)}, u32[]{:S(2)}, u32[]{:S(2)}) async-start(bf16[64,2,64,128]{3,2,1,0:T(8,128)(2,1)} %bitcast.11), calls=%async_computation.1 | async-start | bytes 4194304 | tf_op jit(solution)/shard_map/all_to_all | solution.py:103
  36.0 2.0 copy-start.6
  85.6 56.8 %all-to-all-start.3 = ((bf16[64,2,64,128]{3,2,1,0:T(8,128)(2,1)}), bf16[64,2,64,128]{3,2,1,0:T(8,128)(2,1)}, u32[]{:S(2)}, u32[]{:S(2)}) async-start(bf16[64,2,64,128]{3,2,1,0:T(8,128)(2,1)} %bitcast.17), calls=%async_computation.3 | async-start | bytes 4194304 | tf_op jit(solution)/shard_map/all_to_all | solution.py:146
  92.8 1.8 copy-start
  92.8 1.8 copy-start.8
  142.4 7.4 %copy-start.4 = (bf16[8,16,64,128]{3,2,1,0:T(8,128)(2,1)S(1)}, bf16[8,16,64,128]{3,2,1,0:T(8,128)(2,1)}, u32[]{:S(2)}) copy-start(bf16[8,16,64,128]{3,2,1,0:T(8,128)(2,1)} %get-tuple-element.271) | copy-start | bytes 6291460
  142.4 191.9 %all-to-all-start.2 = ((bf16[64,2,64,128]{3,2,1,0:T(8,128)(2,1)}), bf16[64,2,64,128]{3,2,1,0:T(8,128)(2,1)}, u32[]{:S(2)}, u32[]{:S(2)}) async-start(bf16[64,2,64,128]{3,2,1,0:T(8,128)(2,1)} %bitcast.132), calls=%async_computation.2 | async-start | bytes 4194304 | tf_op jit(solution)/shard_map/all_to_all | solution.py:139
  165.2 5.6 %copy-start.1 = (f32[8,256,256]{2,0,1:T(8,128)S(1)}, f32[8,256,256]{2,0,1:T(8,128)}, u32[]{:S(2)}) copy-start(f32[8,256,256]{2,0,1:T(8,128)} %get-tuple-element.618) | copy-start | bytes 6291460 | tf_op jit(solution)/shard_map/while
  175.8 1.3 copy-start.2
  187.7 5.6 %copy-start.1 = (f32[8,256,256]{2,0,1:T(8,128)S(1)}, f32[8,256,256]{2,0,1:T(8,128)}, u32[]{:S(2)}) copy-start(f32[8,256,256]{2,0,1:T(8,128)} %get-tuple-element.618) | copy-start | bytes 6291460 | tf_op jit(solution)/shard_map/while
  198.2 1.3 copy-start.2
  210.1 5.6 %copy-start.1 = (f32[8,256,256]{2,0,1:T(8,128)S(1)}, f32[8,256,256]{2,0,1:T(8,128)}, u32[]{:S(2)}) copy-start(f32[8,256,256]{2,0,1:T(8,128)} %get-tuple-element.618) | copy-start | bytes 6291460 | tf_op jit(solution)/shard_map/while
  220.7 1.3 copy-start.2
  232.6 5.6 %copy-start.1 = (f32[8,256,256]{2,0,1:T(8,128)S(1)}, f32[8,256,256]{2,0,1:T(8,128)}, u32[]{:S(2)}) copy-start(f32[8,256,256]{2,0,1:T(8,128)} %get-tuple-element.618) | copy-start | bytes 6291460 | tf_op jit(solution)/shard_map/while
  243.1 1.3 copy-start.2
  255.0 5.6 %copy-start.1 = (f32[8,256,256]{2,0,1:T(8,128)S(1)}, f32[8,256,256]{2,0,1:T(8,128)}, u32[]{:S(2)}) copy-start(f32[8,256,256]{2,0,1:T(8,128)} %get-tuple-element.618) | copy-start | bytes 6291460 | tf_op jit(solution)/shard_map/while
  277.5 5.6 %copy-start.1 = (f32[8,256,256]{2,0,1:T(8,128)S(1)}, f32[8,256,256]{2,0,1:T(8,128)}, u32[]{:S(2)}) copy-start(f32[8,256,256]{2,0,1:T(8,128)} %get-tuple-element.618) | copy-start | bytes 6291460 | tf_op jit(solution)/shard_map/while
  300.0 5.6 %copy-start.1 = (f32[8,256,256]{2,0,1:T(8,128)S(1)}, f32[8,256,256]{2,0,1:T(8,128)}, u32[]{:S(2)}) copy-start(f32[8,256,256]{2,0,1:T(8,128)} %get-tuple-element.618) | copy-start | bytes 6291460 | tf_op jit(solution)/shard_map/while
  322.4 5.6 %copy-start.1 = (f32[8,256,256]{2,0,1:T(8,128)S(1)}, f32[8,256,256]{2,0,1:T(8,128)}, u32[]{:S(2)}) copy-start(f32[8,256,256]{2,0,1:T(8,128)} %get-tuple-element.618) | copy-start | bytes 6291460 | tf_op jit(solution)/shard_map/while
  334.3 10.6 %copy-start.3 = (f32[8,256,256]{2,0,1:T(8,128)S(1)}, f32[8,256,256]{2,0,1:T(8,128)}, u32[]{:S(2)}) copy-start(f32[8,256,256]{2,0,1:T(8,128)} %get-tuple-element.274) | copy-start | bytes 6291460
  334.3 165.1 %all-to-all-start.4 = ((bf16[64,2,64,128]{3,2,1,0:T(8,128)(2,1)}), bf16[64,2,64,128]{3,2,1,0:T(8,128)(2,1)}, u32[]{:S(2)}, u32[]{:S(2)}) async-start(bf16[64,2,64,128]{3,2,1,0:T(8,128)(2,1)} %bitcast.133), calls=%async_computation.4 | async-start | bytes 4194304 | tf_op jit(solution)/shard_map/all_to_all | solution.py:178
  (4 other events, 5.3 us)
where the time goes:
time: 507 us; the launch traced here: 502 us
  blocking collectives  150 us (30%)
  matrix products  115 us (23%)
  local copies, waits for them, and re-layouts  103 us (20%)
  waiting for transfers between devices  58.5 us (12%)
  starting transfers between devices  47.2 us (9%)
  other arithmetic  27.2 us (5%)
    psum x1, blocking collectives, body(): bias_grad = lax.psum(bias_local, ('dp', 'pool'))  150 us
    concatenate x8, local copies, waits for them, and re-layouts, block_backward(): kv_grad = jnp.concatenate([key_gradient, value_gradient], axis=-1)  45.2 us
    all_to_all x1, waiting for transfers between devices, body(): lax.all_to_all(query_send.reshape(npool, capacity, span, width), 'pool',...  42.8 us
    dot_general x8, matrix products, block_backward(): jnp.einsum('sn,skd->nkd', selector, kv_grad, precision=lax.Precision.HIGH...  39.3 us
    dot_general x16, matrix products, block_scores(): jnp.einsum('sqd,skd->sqk', query_block, neighbour_keys, preferred_element...  24 us
    concatenate x8, other arithmetic, block_backward(): kv_grad = jnp.concatenate([key_gradient, value_gradient], axis=-1)  17.9 us
    all_to_all x1, starting transfers between devices, body(): lax.all_to_all(row_send.reshape(npool, capacity), 'pool', split_axis=0, c...  14.5 us
    all_to_all x1, waiting for transfers between devices, body(): lax.all_to_all(cot_send, 'pool', split_axis=0, concat_axis=0, tiled=True)  12.4 us
  transfers between devices with their start and end apart: 5, of which 3 were waited for; matrix products, arithmetic and copies ran while one was open for 45% of the time, Pallas kernels for 0%

commit v1 on v0

v1 whole, which is shorter than its diff:
```python
import functools

import jax
import jax.numpy as jnp
from jax import lax
from jax.experimental import pallas as pl
from jax.experimental.pallas import tpu as pltpu
from jax.sharding import PartitionSpec as P

MESH = pl.DeviceIdType.MESH
NEIGH = 2
CAP = 2
GROUP = 7
NX = 4


def kernel(
    ndp, npool, nx, ny,
    idx_ref, slot_ref, lens_ref, meta_ref, q_ref, c_ref, table_ref, bias_ref,
    att_ref, dq_ref, grad_ref, bgrad_ref,
    meta_got, meta_s, send, recv, back, ret, dsb, wb, rhs, acc, bacc,
    plane, planes,
    meta_ss, meta_rs, meta_cs, send_ss, send_rs, ret_ss, ret_rs,
    b_ss, b_rs, z_ss, z_rs,
):
    dp, me = lax.axis_index("dp"), lax.axis_index("pool")
    core, cx, cy = me % 2, (me // 2) % nx, me // (2 * nx)
    nspans, span, width = q_ref.shape
    nsets, keys, _ = table_ref.shape
    scale = width ** -0.5

    def offsets(s):
        r = s // 2
        b, a = r % ny, r // ny
        return s % 2, (b + a) % nx, (3 * b) % ny

    def place(c, x, y):
        return (y * nx + x) * 2 + c

    def target(s):
        dc, dx, dy = offsets(s)
        return place((core + dc) % 2, (cx + dx) % nx, (cy + dy) % ny)

    def origin(s):
        dc, dx, dy = offsets(s)
        return place((core + 2 - dc) % 2, (cx + nx - dx) % nx, (cy + ny - dy) % ny)

    def remote(src, dst, ss, rs, where):
        return pltpu.make_async_remote_copy(
            src_ref=src, dst_ref=dst, send_sem=ss, recv_sem=rs,
            device_id=where, device_id_type=MESH,
        )

    def each(lo, hi, f):
        def step(i, carry):
            f(i)
            return carry
        lax.fori_loop(lo, hi, step, 0)

    def added(ref, count):
        return lax.fori_loop(0, count, lambda i, total: total + ref[i], jnp.zeros((8, keys), jnp.float32))

    barrier = pltpu.get_barrier_semaphore()
    each(1, npool, lambda s: pl.semaphore_signal(
        barrier, inc=1, device_id={"pool": target(s)}, device_id_type=MESH))
    each(1, ndp, lambda s: pl.semaphore_signal(
        barrier, inc=1, device_id={"dp": (dp + s) % ndp}, device_id_type=MESH))
    pl.semaphore_wait(barrier, npool - 1 + ndp - 1)

    def meta_copy(peer, mine):
        return remote(meta_ref.at[peer], meta_got.at[mine], meta_ss.at[peer], meta_rs.at[mine], {"pool": peer})

    each(1, npool, lambda s: meta_copy(target(s), me).start())
    meta_got[me] = meta_ref[me]

    def pack(peer, buf):
        for k in range(CAP):
            i = idx_ref[peer * CAP + k]
            buf[peer, k, 0] = q_ref[i]
            buf[peer, k, 1] = c_ref[i]

    def data_copy(peer, mine):
        return remote(send.at[peer], recv.at[mine], send_ss.at[peer], send_rs.at[mine], {"pool": peer})

    def ret_copy(peer, mine):
        return remote(back.at[peer], ret.at[mine], ret_ss.at[peer], ret_rs.at[mine], {"pool": peer})

    def out(s):
        peer = target(s)
        pack(peer, send)
        data_copy(peer, me).start()

    each(1, npool, out)
    pack(me, recv)

    acc[...] = jnp.zeros_like(acc)
    bacc[...] = jnp.zeros_like(bacc)
    each(1, npool, lambda s: meta_copy(origin(s), origin(s)).wait_recv())
    to_scalar = pltpu.make_async_copy(meta_got, meta_s, meta_cs)
    to_scalar.start()
    to_scalar.wait()

    def attend(src, at, dest):
        total = jnp.zeros((8, keys), jnp.float32)
        slots = lax.broadcasted_iota(jnp.int32, (1, keys), 1)
        part = keys // NEIGH
        first, position, bias_rows = slots < part, slots % part, bias_ref[...]
        for k in range(CAP):
            row = meta_s[src, 0, k]
            used = row >= 0
            pick = jnp.maximum(row, 0)
            q, c = recv[src, k, 0], recv[src, k, 1]
            kv = table_ref[pick]
            kk, vv = kv[:, :width], kv[:, width:]
            scores = lax.dot_general(q, kk, (((1,), (1,)), ((), ())), preferred_element_type=jnp.float32)
            limit = jnp.where(first, lens_ref[pick * NEIGH], lens_ref[pick * NEIGH + 1])
            extra = jnp.where(position < limit, bias_rows, -1e30)
            scores = scores * scale + extra
            peak = jnp.max(scores, axis=1, keepdims=True)
            e = jnp.exp(scores - peak)
            probs = e / jnp.sum(e, axis=1, keepdims=True)
            weights = probs.astype(jnp.bfloat16)
            att = jnp.dot(weights, vv, preferred_element_type=jnp.float32).astype(jnp.bfloat16)
            delta = jnp.sum(c.astype(jnp.float32) * att.astype(jnp.float32), axis=1, keepdims=True)
            dw = lax.dot_general(c, vv, (((1,), (1,)), ((), ())), preferred_element_type=jnp.float32)
            ds = probs * (dw - delta)
            total = total + jnp.where(used, jnp.sum(ds.reshape(span // 8, 8, keys), axis=0), 0.0)
            dss = (ds * scale).astype(jnp.bfloat16)
            dest[src, k, 0] = att
            dest[src, k, 1] = jnp.dot(dss, kk, preferred_element_type=jnp.float32).astype(jnp.bfloat16)
            rows = pl.ds(pl.multiple_of((at * CAP + k) * span, span), span)
            dsb[rows, :] = dss
            wb[rows, :] = weights
        bacc[...] += total

    def gradients(source, count):
        size = count * CAP * span
        turned = (dsb[pl.ds(0, size), :].T, wb[pl.ds(0, size), :].T)
        for j in range(nsets // 2):
            for which in range(2):
                def fill(t, which=which, j=j):
                    src = source(t)
                    for k in range(CAP):
                        row = meta_s[src, 0, k]
                        x = recv[src, k, which]
                        rows = pl.ds(pl.multiple_of((t * CAP + k) * span, span), span)
                        rhs[rows, :width] = jnp.where(row == 2 * j, x, jnp.zeros_like(x))
                        rhs[rows, width:] = jnp.where(row == 2 * j + 1, x, jnp.zeros_like(x))
                each(0, count, fill)
                acc[j, which] += jnp.dot(turned[which], rhs[pl.ds(0, size), :], preferred_element_type=jnp.float32)

    attend(me, 0, ret)
    gradients(lambda t: me, 1)

    def batch(i):
        def one(t):
            src = origin(1 + i * GROUP + t)
            data_copy(src, src).wait_recv()
            attend(src, t, back)
            ret_copy(src, me).start()
        each(0, GROUP, one)
        gradients(lambda t: origin(1 + i * GROUP + t), GROUP)

    each(0, (npool - 1) // GROUP, batch)

    plane[me] = bacc[...]

    def plane_copy(peer, mine):
        return remote(bacc, plane.at[mine], b_ss.at[peer], b_rs.at[mine], {"pool": peer})

    each(1, npool, lambda s: plane_copy(target(s), me).start())

    for j in range(nsets // 2):
        for which in range(2):
            for h in range(2):
                grad_ref[2 * j + h, :, which * width:(which + 1) * width] = (
                    acc[j, which, :, h * width:(h + 1) * width].astype(jnp.bfloat16))

    each(1, npool, lambda s: plane_copy(origin(s), origin(s)).wait_recv())
    planes[dp] = added(plane, npool)

    def z_copy(peer, mine):
        return remote(planes.at[dp], planes.at[mine], z_ss.at[peer], z_rs.at[mine], {"dp": peer})

    each(1, ndp, lambda s: z_copy((dp + s) % ndp, dp).start())
    each(1, ndp, lambda s: z_copy((dp + s) % ndp, (dp + s) % ndp).wait_recv())
    bgrad_ref[...] = jnp.sum(added(planes, ndp), axis=0, keepdims=True)

    each(1, npool, lambda s: ret_copy(target(s), target(s)).wait_recv())

    def place_out(i):
        slot = slot_ref[i]
        o, k = slot // CAP, slot % CAP
        att_ref[i] = ret[o, k, 0]
        dq_ref[i] = ret[o, k, 1]

    each(0, nspans, place_out)

    def drain(s):
        peer = target(s)
        meta_copy(peer, me).wait_send()
        data_copy(peer, me).wait_send()
        ret_copy(peer, me).wait_send()
        plane_copy(peer, me).wait_send()

    each(1, npool, drain)
    each(1, ndp, lambda s: z_copy((dp + s) % ndp, dp).wait_send())


def body(ndp, npool, nx, ny, queries, cotangent, owner, row, table, lengths, bias):
    nspans = owner.shape[0]
    width = queries.shape[1]
    span = queries.shape[0] // nspans
    nsets, keys, _ = table.shape
    own = owner[:, 0]
    order = jnp.arange(nspans, dtype=jnp.int32)
    rank = jnp.sum(((own[:, None] == own[None, :]) & (order[None, :] < order[:, None])).astype(jnp.int32), axis=1)
    slot = own * CAP + rank
    slots = jnp.arange(npool * CAP, dtype=jnp.int32)
    hit = (slot[None, :] == slots[:, None]).astype(jnp.int32)
    idx = jnp.sum(hit * order[None, :], axis=1)
    sets = jnp.sum(hit * (row + 1)[None, :], axis=1) - 1
    meta = jnp.pad(sets.reshape(npool, 1, CAP), ((0, 0), (0, 0), (0, 128 - CAP)))
    bf, f32 = jnp.bfloat16, jnp.float32
    vmem = pl.BlockSpec(memory_space=pltpu.VMEM)
    smem = pl.BlockSpec(memory_space=pltpu.SMEM)
    dma = pltpu.SemaphoreType.DMA
    rows = GROUP * CAP * span
    att, dq, grad, bgrad = pl.pallas_call(
        functools.partial(kernel, ndp, npool, nx, ny),
        out_shape=(
            jax.ShapeDtypeStruct((nspans, span, width), bf),
            jax.ShapeDtypeStruct((nspans, span, width), bf),
            jax.ShapeDtypeStruct(table.shape, bf),
            jax.ShapeDtypeStruct((1, keys), f32),
        ),
        in_specs=[smem, smem, smem, vmem, vmem, vmem, vmem, vmem],
        out_specs=(vmem, vmem, vmem, vmem),
        scratch_shapes=[
            pltpu.VMEM((npool, 1, 128), jnp.int32),
            pltpu.SMEM((npool, 1, 128), jnp.int32),
            pltpu.VMEM((npool, CAP, 2, span, width), bf),
            pltpu.VMEM((npool, CAP, 2, span, width), bf),
            pltpu.VMEM((npool, CAP, 2, span, width), bf),
            pltpu.VMEM((npool, CAP, 2, span, width), bf),
            pltpu.VMEM((rows, keys), bf),
            pltpu.VMEM((rows, keys), bf),
            pltpu.VMEM((rows, 2 * width), bf),
            pltpu.VMEM((nsets // 2, 2, keys, 2 * width), f32),
            pltpu.VMEM((8, keys), f32),
            pltpu.VMEM((npool, 8, keys), f32),
            pltpu.VMEM((ndp, 8, keys), f32),
            dma((npool,)), dma((npool,)), dma(()),
            dma((npool,)), dma((npool,)),
            dma((npool,)), dma((npool,)),
            dma((npool,)), dma((npool,)),
            dma((ndp,)), dma((ndp,)),
        ],
        compiler_params=pltpu.CompilerParams(
            collective_id=0, has_side_effects=True, vmem_limit_bytes=56 * 1024 * 1024),
    )(
        idx, slot, lengths.reshape(-1), meta,
        queries.reshape(nspans, span, width), cotangent.reshape(nspans, span, width),
        table, bias,
    )
    return att.reshape(queries.shape), dq.reshape(queries.shape), grad, bgrad


def solution(mesh):
    ndp, npool = mesh.shape["dp"], mesh.shape["pool"]
    nx = NX
    ny = npool // (2 * nx)
    pool = P(("dp", "pool"), None)
    cube = P(("dp", "pool"), None, None)
    return jax.shard_map(
        functools.partial(body, ndp, npool, nx, ny),
        mesh=mesh,
        in_specs=(pool, pool, pool, P(("dp", "pool")), cube, pool, P()),
        out_specs=(pool, pool, cube, P()),
        check_vma=False,
    )
```

time: 507 us -> 250 us (0.49)
  Pallas kernels: 0 us -> 240 us
  blocking collectives: 150 us -> 0 us
  matrix products: 115 us -> 0 us
  local copies, waits for them, and re-layouts: 103 us -> 8.08 us
  waiting for transfers between devices: 58.5 us -> 0 us
  starting transfers between devices: 47.2 us -> 0 us
  other arithmetic: 27.2 us -> 0.78 us
    pallas_call x0 -> x1, Pallas kernels: none -> 240 us  [body(): pl.pallas_call(functools.partial(kernel, ndp, npool, nx, ny), out_shape=(...]
    psum x1 -> x0, blocking collectives: 150 us -> none  [body(): bias_grad = lax.psum(bias_local, ('dp', 'pool'))]
    dot_general x64 -> x0, matrix products: 115 us -> none  [the longest x8 39.3 us: block_backward(): jnp.einsum('sn,skd->nkd', selector, kv_grad, precision=lax.Precision.HIGH...]
    all_to_all x5 -> x0, waiting for transfers between devices: 58.5 us -> none  [the longest x1 42.8 us: body(): lax.all_to_all(query_send.reshape(npool, capacity, span, width), 'pool',...]
    all_to_all x5 -> x0, starting transfers between devices: 47.2 us -> none  [the longest x1 14.5 us: body(): lax.all_to_all(row_send.reshape(npool, capacity), 'pool', split_axis=0, c...]
    concatenate x8 -> x0, local copies, waits for them, and re-layouts: 45.2 us -> none  [block_backward(): kv_grad = jnp.concatenate([key_gradient, value_gradient], axis=-1)]
    gather x34 -> x0, local copies, waits for them, and re-layouts: 25.9 us -> none  [the longest x8 5.46 us: forward_block(): kv_blk = table[picked_blk]]
    concatenate x8 -> x0, other arithmetic: 17.9 us -> none  [block_backward(): kv_grad = jnp.concatenate([key_gradient, value_gradient], axis=-1)]
  transfers between devices with their start and end apart: 5 -> 0, of which waited for: 3 -> 0; matrix products, arithmetic and copies ran while one was open for 45% -> 0% of each run, Pallas kernels for 0% -> 0%
where the time goes in v1:
time: 250 us; the launch traced here: 249 us
  Pallas kernels  240 us (96%)
  local copies, waits for them, and re-layouts  8.08 us (3%)
    pallas_call x1, Pallas kernels, body(): pl.pallas_call(functools.partial(kernel, ndp, npool, nx, ny), out_shape=(...  240 us
    unnamed x19, local copies, waits for them, and re-layouts  6.71 us

profile of v1, /device:TPU:1, one launch (start us, length us, event | category | flops | bytes accessed | tf_op | source)
XLA Modules:
  0.0 249.2 jit_solution(3381105633461419057)
XLA Ops:
  0.6 0.0 copy-start.5
  0.6 0.6 copy-done.5
  1.3 0.0 copy-start.6
  1.3 0.2 convert_reduce_fusion
  1.5 0.5 copy-done.6
  1.9 0.5 copy-done.2
  2.5 0.6 select_reduce_fusion
  3.1 0.0 copy-start.3
  3.1 0.7 copy-done.3
  3.7 0.1 copy.15
  3.8 0.6 reshape.46.lens_ref
  4.4 0.1 sub.7
  4.5 0.6 pad.4.meta_ref
  5.2 239.7 %shard_map.102 = (bf16[32,64,128]{2,1,0:T(8,128)(2,1)}, bf16[32,64,128]{2,1,0:T(8,128)(2,1)}, bf16[8,256,256]{2,1,0:T(8,128)(2,1)}, f32[1,256]{1,0:T(1,128)}) custom-call(s32[128]{0:T(128)} %get-tuple-element.13.idx_ref, s32[32]{0:T(128)} %copy-done.2, s32[16]{0:T(128)} %reshape.46.lens_ref, s32[64,1,128]{2,1,0:T(1,128)} %pad.4.meta_ref, ...), custom_call_target="tpu_custom_call" | custom-call | tf_op jit(solution)/shard_map/pallas_call | solution.py:229
  244.9 0.0 copy-start.1
  244.9 0.0 copy-start
  244.9 2.0 copy.21
  246.9 0.0 copy-done.1
  246.9 0.8 copy.22
  247.7 0.0 copy-done
  247.7 0.0 copy-start.4
  247.7 1.0 copy.23
  248.7 0.0 copy-done.4
  248.7 0.6 copy.24
  (3 shorter events, 0.0 us)
Async XLA Ops:
  0.6 0.7 copy-start.5
  1.3 0.7 copy-start.6
  1.9 0.5 copy-start.2
  3.1 0.7 copy-start.3
  244.9 2.0 copy-start.1
  244.9 2.8 %copy-start = (bf16[8,256,256]{2,1,0:T(8,128)(2,1)S(1)}, bf16[8,256,256]{2,1,0:T(8,128)(2,1)}, u32[]{:S(2)}) copy-start(bf16[8,256,256]{2,1,0:T(8,128)(2,1)} %get-tuple-element.22) | copy-start | bytes 3145732
  247.7 1.0 copy-start.4

commit v2 on v1

--- a/solution.py
+++ b/solution.py
@@ -10,11 +10,371 @@
 MESH = pl.DeviceIdType.MESH
 NEIGH = 2
 CAP = 2
+LEAN = 2
 GROUP = 7
 NX = 4
 
 
-def kernel(
+def lean_kernel(
+    ndp, npool, nx, ny,
+    lens_ref, own_ref, row_ref, q_ref, c_ref, table_ref, bias_ref,
+    att_ref, dq_ref, grad_ref, bgrad_ref, over_ref,
+    plan_v, plan_s, mine_v, above_v, above_s, aside_v, meta_v, meta_s,
+    send, recv, back, ret, osend, orecv, oback, rsend, rret,
+    dsb, wb, rhs, acc, bacc, rowsum, colsum, zsum,
+    copy_sem, m_ss, m_rs, n_ss, n_rs, send_ss, send_rs, ret_ss, ret_rs,
+    o_ss, o_rs, r_ss, r_rs, rb_ss, rb_rs, ob_ss, ob_rs,
+    br_ss, br_rs, bc_ss, bc_rs, z_ss, z_rs,
+):
+    dp, me = lax.axis_index("dp"), lax.axis_index("pool")
+    nrow = 2 * nx
+    core, cx, cy, spot = me % 2, (me // 2) % nx, me // nrow, me % nrow
+    nspans, span, width = q_ref.shape
+    nsets, keys, _ = table_ref.shape
+    part = keys // NEIGH
+    scale = width ** -0.5
+
+    def offsets(s):
+        r = s // 2
+        b, a = r % ny, r // ny
+        return s % 2, (b + a) % nx, (3 * b) % ny
+
+    def place(c, x, y):
+        return (y * nx + x) * 2 + c
+
+    def target(s):
+        dc, dx, dy = offsets(s)
+        return place((core + dc) % 2, (cx + dx) % nx, (cy + dy) % ny)
+
+    def origin(s):
+        dc, dx, dy = offsets(s)
+        return place((core + 2 - dc) % 2, (cx + nx - dx) % nx, (cy + ny - dy) % ny)
+
+    def beside(s):
+        return ((cx + s // 2) % nx) * 2 + (core + s) % 2
+
+    def above(s):
+        return (cy + 3 * s) % ny
+
+    def in_row(m):
+        return cy * nrow + m
+
+    def in_column(y):
+        return y * nrow + spot
+
+    def remote(src, dst, ss, rs, where):
+        return pltpu.make_async_remote_copy(
+            src_ref=src, dst_ref=dst, send_sem=ss, recv_sem=rs,
+            device_id=where, device_id_type=MESH,
+        )
+
+    def each(lo, hi, f):
+        def step(i, carry):
+            f(i)
+            return carry
+        lax.fori_loop(lo, hi, step, 0)
+
+    def ask_copy(y, mine):
+        return remote(mine_v.at[y], above_v.at[mine], m_ss.at[y], m_rs.at[mine], {"pool": in_column(y)})
+
+    def tell_copy(m, mine):
+        return remote(aside_v.at[m], meta_v.at[mine], n_ss.at[m], n_rs.at[mine], {"pool": in_row(m)})
+
+    def data_copy(peer, mine):
+        return remote(send.at[peer], recv.at[mine], send_ss.at[peer], send_rs.at[mine], {"pool": peer})
+
+    def ret_copy(peer, mine):
+        return remote(back.at[peer], ret.at[mine], ret_ss.at[peer], ret_rs.at[mine], {"pool": peer})
+
+    def over_copy(y, mine):
+        return remote(osend.at[y], orecv.at[mine], o_ss.at[y], o_rs.at[mine], {"pool": in_column(y)})
+
+    def row_copy(m, mine):
+        return remote(rsend.at[m], recv.at[pl.ds(npool + mine * ny, ny)], r_ss.at[m], r_rs.at[mine], {"pool": in_row(m)})
+
+    def row_back(m, mine):
+        return remote(back.at[pl.ds(npool + m * ny, ny)], rret.at[mine], rb_ss.at[m], rb_rs.at[mine], {"pool": in_row(m)})
+
+    def over_back(y, mine):
+        return remote(oback.at[y], ret.at[pl.ds(npool + mine * LEAN, LEAN)], ob_ss.at[y], ob_rs.at[mine],
+                      {"pool": in_column(y)})
+
+    def row_sum(m, mine):
+        return remote(bacc, rowsum.at[mine], br_ss.at[m], br_rs.at[mine], {"pool": in_row(m)})
+
+    def col_sum(y, mine):
+        return remote(colsum.at[cy], colsum.at[mine], bc_ss.at[y], bc_rs.at[mine], {"pool": in_column(y)})
+
+    def z_sum(z, mine):
+        return remote(zsum.at[dp], zsum.at[mine], z_ss.at[z], z_rs.at[mine], {"dp": z})
+
+    def local(src, dst, k):
+        copy = pltpu.make_async_copy(src, dst, copy_sem.at[k])
+        copy.start()
+        copy.wait()
+
+    barrier = pltpu.get_barrier_semaphore()
+    each(1, npool, lambda s: pl.semaphore_signal(
+        barrier, inc=1, device_id={"pool": target(s)}, device_id_type=MESH))
+    each(1, ndp, lambda s: pl.semaphore_signal(
+        barrier, inc=1, device_id={"dp": (dp + s) % ndp}, device_id_type=MESH))
+
+    def plan():
+        bits, n = nrow.bit_length() - 1, nspans
+        one, many = (lambda x: jnp.where(x, 1, 0)), (lambda x, axis: jnp.sum(x, axis=axis, keepdims=True))
+        order_s, order_l = (lax.broadcasted_iota(jnp.int32, shape, axis) for shape, axis in (((n, 1), 0), ((1, n), 1)))
+        lanes = lax.broadcasted_iota(jnp.int32, (1, 128), 1)
+        peers = lax.broadcasted_iota(jnp.int32, (npool, 1), 0)
+        own_s, row_l = own_ref[...], row_ref[...]
+        own_l = many(one(order_s == order_l) * own_s, 0)
+        same = one(own_s == own_l)
+        rank_s, rank_l = many(same * one(order_l < order_s), 1), many(same * one(order_s < order_l), 0)
+        home_s, home_l, local_l = own_s >> bits, own_l >> bits, own_l & (nrow - 1)
+        near = one(home_s == home_l)
+        place_s = many(near * one(own_l < own_s) * rank_l, 1)
+        place_l = many(near * one(own_s < own_l) * rank_s, 0)
+        carried_s, carried_l = rank_s * one(place_s < LEAN), rank_l * one(place_l < LEAN)
+        slot_s = rank_s * (npool + home_s * LEAN + jnp.minimum(place_s, LEAN - 1)) + (1 - rank_s) * own_s
+        taken_s = (1 - rank_s) + carried_s
+        plan_v[0:1, :] = many(one(slot_s == lanes) * (taken_s * order_s), 0)
+        plan_v[1:2, :] = many(one(order_s == lanes) * slot_s, 0)
+        at_peer, at_row = one(own_l == peers), one(home_l == (peers >> bits))
+        fields = [
+            many(at_peer * ((1 - rank_l) * (row_l + 1)), 1) - 1,
+            many(at_peer * (carried_l * (row_l + 1)), 1) - 1,
+            many(at_peer * (carried_l * place_l), 1),
+        ] + [many(at_row * (carried_l * one(place_l == j) * local_l), 1) for j in range(LEAN)]
+        meta = jnp.zeros((npool, 128), jnp.int32)
+        for k, field in enumerate(fields):
+            meta = jnp.where(lanes == k, field, meta)
+        mine_v[...] = meta.reshape(ny, nrow, 128)
+        over = many(rank_l * one(place_l >= LEAN), 1).astype(jnp.float32)
+        bacc[:, :keys] = jnp.zeros((8, keys), jnp.float32)
+        bacc[:, keys:] = jnp.broadcast_to(over, (8, 128))
+        local(plan_v, plan_s, 0)
+
+    def pack_over(y, buf):
+        for j in range(LEAN):
+            i = jnp.clip(plan_s[0, npool + y * LEAN + j], 0, nspans - 1)
+            buf[y, j, 0] = q_ref[i]
+            buf[y, j, 1] = c_ref[i]
+
+    def pack(peer, buf):
+        i = jnp.clip(plan_s[0, peer], 0, nspans - 1)
+        buf[peer, 0] = q_ref[i]
+        buf[peer, 1] = c_ref[i]
+
+    plan()
+    each(1, ny, lambda s: pack_over(above(s), osend))
+    pack_over(cy, orecv)
+    above_v[cy] = mine_v[cy]
+    pl.semaphore_wait(barrier, npool - 1 + ndp - 1)
+
+    each(1, ny, lambda s: ask_copy(above(s), cy).start())
+    each(1, ny, lambda s: over_copy(above(s), cy).start())
+
+    def out(s):
+        peer = target(s)
+        pack(peer, send)
+        data_copy(peer, me).start()
+
+    stride = (2 * npool // 3) // (nrow - 1)
+    ahead = npool - stride * (nrow - 1)
+    each(1, ahead, out)
+    pack(me, recv)
+
+    each(1, ny, lambda s: ask_copy(above(s), above(s)).wait_recv())
+    for m in range(nrow):
+        for y in range(ny):
+            aside_v[m, y:y + 1, :] = above_v[y, m:m + 1, :]
+    each(1, nrow, lambda s: tell_copy(beside(s), spot).start())
+    meta_v[spot] = aside_v[spot]
+    local(above_v, above_s, 1)
+    acc[...] = jnp.zeros_like(acc)
+
+    def fill(m, put):
+        def one(y):
+            j = jnp.clip(above_s[y, m, 2], 0, LEAN - 1)
+            put(y, orecv[y, j])
+        each(0, ny, one)
+
+    def relay_in(s):
+        m = beside(s)
+        def put(y, x):
+            rsend[m, y] = x
+        fill(m, put)
+        row_copy(m, spot).start()
+        each(ahead + (s - 1) * stride, ahead + s * stride, out)
+
+    each(1, ny, lambda s: over_copy(above(s), above(s)).wait_recv())
+    each(1, nrow, relay_in)
+    def put(y, x):
+        recv[npool + spot * ny + y] = x
+    fill(spot, put)
+    each(1, nrow, lambda s: tell_copy(beside(s), beside(s)).wait_recv())
+    local(meta_v, meta_s, 2)
+
+    def relay_out():
+        def keep(y):
+            rret[spot, y] = back[npool + spot * ny + y]
+        each(0, ny, keep)
+        each(1, nrow, lambda s: row_back(beside(s), beside(s)).wait_recv())
+
+        def go(s):
+            y = above(s)
+            for j in range(LEAN):
+                m = jnp.clip(above_s[y, 0, 3 + j], 0, nrow - 1)
+                oback[y, j] = rret[m, y]
+            over_back(y, cy).start()
+
+        each(1, ny, go)
+        for j in range(LEAN):
+            m = jnp.clip(above_s[cy, 0, 3 + j], 0, nrow - 1)
+            ret[npool + cy * LEAN + j] = rret[m, cy]
+
+    def attend(items):
+        count = len(items)
+        slots = lax.broadcasted_iota(jnp.int32, (1, keys), 1)
+        first, position, bias_rows = slots < part, slots % part, bias_ref[...]
+        blank = jnp.zeros((span, width), jnp.bfloat16)
+        kvs, both = [], []
+        for source, row, dest in items:
+            q, c = source[0], source[1]
+            kv = table_ref[jnp.clip(row, 0, nsets - 1)]
+            wide = jnp.concatenate(
+                [jnp.concatenate([q, blank], axis=1), jnp.concatenate([blank, c], axis=1)], axis=0)
+            kvs.append(kv)
+            both.append(lax.dot_general(wide, kv, (((1,), (1,)), ((), ())), preferred_element_type=jnp.float32))
+        total = jnp.zeros((8, keys), jnp.float32)
+        probs = []
+        for t, (source, row, dest) in enumerate(items):
+            pick = jnp.clip(row, 0, nsets - 1)
+            limit = jnp.where(first, lens_ref[pick, 0], lens_ref[pick, 1])
+            extra = jnp.where(position < limit, bias_rows, -1e30)
+            scores = both[t][:span] * scale + extra
+            e = jnp.exp(scores - jnp.max(scores, axis=1, keepdims=True))
+            probs.append(e * (1.0 / jnp.sum(e, axis=1, keepdims=True)))
+            wb[t * span:(t + 1) * span, :] = probs[t].astype(jnp.bfloat16)
+        deltas = []
+        for t, (source, row, dest) in enumerate(items):
+            att = jnp.dot(probs[t].astype(jnp.bfloat16), kvs[t][:, width:], preferred_element_type=jnp.float32)
+            att = att.astype(jnp.bfloat16)
+            dest[0] = att
+            deltas.append(jnp.sum(source[1].astype(jnp.float32) * att.astype(jnp.float32), axis=1, keepdims=True))
+        for t, (source, row, dest) in enumerate(items):
+            ds = probs[t] * (both[t][span:] - deltas[t])
+            total = total + jnp.where(row >= 0, jnp.sum(ds.reshape(span // 8, 8, keys), axis=0), 0.0)
+            dss = (ds * scale).astype(jnp.bfloat16)
+            dsb[t * span:(t + 1) * span, :] = dss
+            dest[1] = jnp.dot(dss, kvs[t][:, :width], preferred_element_type=jnp.float32).astype(jnp.bfloat16)
+        bacc[:, :keys] += total
+        size = count * span
+        for which, left in ((0, dsb), (1, wb)):
+            for t, (source, row, dest) in enumerate(items):
+                x = source[which]
+                for n in range(nsets):
+                    rhs[which, t * span:(t + 1) * span, n * width:(n + 1) * width] = jnp.where(row == n, x, blank)
+            acc[which] += lax.dot_general(
+                left[:size, :], rhs[which, :size, :], (((0,), (0,)), ((), ())), preferred_element_type=jnp.float32)
+
+    cut, last = 3 * nrow // 2, 2 * nrow
+
+    def batch(k):
+        late = k // cut
+        second = (1 - late) * ((k % 3 + 1) // 2)
+        b = (1 - late) * (k // 3) + late * (k - nrow)
+        m = beside((1 - late) * second * (2 * (k // 3) + k % 3 - 1))
+
+        @pl.when(k == last - 2)
+        def _():
+            relay_out()
+
+        def wait_first(t):
+            src = origin(b * ny + t)
+
+            @pl.when((1 - second) * (b * ny + t) > 0)
+            def _():
+                data_copy(src, src).wait_recv()
+
+        each(0, ny, wait_first)
+        aside = (spot + nrow - m) % nrow
+
+        @pl.when(second * aside > 0)
+        def _():
+            row_copy(m, m).wait_recv()
+
+        items = []
+        for t in range(ny):
+            src = origin(b * ny + t)
+            at = (1 - second) * src + second * (npool + m * ny + t)
+            row = meta_s[(1 - second) * (src % nrow) + second * m, (1 - second) * (src // nrow) + second * t, second]
+            items.append((recv.at[at], row, back.at[at]))
+        attend(items)
+
+        def send_first(t):
+            src = origin(b * ny + t)
+
+            @pl.when((1 - second) * (b * ny + t) > 0)
+            def _():
+                ret_copy(src, me).start()
+
+        each(0, ny, send_first)
+
+        @pl.when(second * aside > 0)
+        def _():
+            row_back(m, spot).start()
+
+    each(0, last, batch)
+    ret[me] = back[me]
+
+    def added(ref, count):
+        return lax.fori_loop(0, count, lambda i, total: total + ref[i], jnp.zeros(bacc.shape, jnp.float32))
+
+    rowsum[spot] = bacc[...]
+    each(1, nrow, lambda s: row_sum(beside(s), spot).start())
+    for which in range(2):
+        for n in range(nsets):
+            grad_ref[n, :, which * width:(which + 1) * width] = (
+                acc[which, :, n * width:(n + 1) * width].astype(jnp.bfloat16))
+    each(1, nrow, lambda s: row_sum(beside(s), beside(s)).wait_recv())
+    colsum[cy] = added(rowsum, nrow)
+    each(1, ny, lambda s: col_sum(above(s), cy).start())
+    each(1, ny, lambda s: col_sum(above(s), above(s)).wait_recv())
+    zsum[dp] = added(colsum, ny)
+    each(1, ndp, lambda s: z_sum((dp + s) % ndp, dp).start())
+    each(1, ndp, lambda s: z_sum((dp + s) % ndp, (dp + s) % ndp).wait_recv())
+    whole = added(zsum, ndp)
+    bgrad_ref[...] = jnp.sum(whole[:, :keys], axis=0, keepdims=True)
+    over_ref[...] = whole[:, keys:]
+
+    each(1, npool, lambda s: ret_copy(target(s), target(s)).wait_recv())
+    each(1, ny, lambda s: over_back(above(s), above(s)).wait_recv())
+
+    def place_out(i):
+        slot = jnp.clip(plan_s[1, i], 0, npool + ny * LEAN - 1)
+        att_ref[i] = ret[slot, 0]
+        dq_ref[i] = ret[slot, 1]
+
+    each(0, nspans, place_out)
+
+    def drain(s):
+        peer = target(s)
+        data_copy(peer, me).wait_send()
+        ret_copy(peer, me).wait_send()
+
+    each(1, npool, drain)
+    each(1, ny, lambda s: ask_copy(above(s), cy).wait_send())
+    each(1, nrow, lambda s: tell_copy(beside(s), spot).wait_send())
+    each(1, nrow, lambda s: row_sum(beside(s), spot).wait_send())
+    each(1, ny, lambda s: col_sum(above(s), cy).wait_send())
+    each(1, ny, lambda s: over_copy(above(s), cy).wait_send())
+    each(1, ny, lambda s: over_back(above(s), cy).wait_send())
+    each(1, nrow, lambda s: row_copy(beside(s), spot).wait_send())
+    each(1, nrow, lambda s: row_back(beside(s), spot).wait_send())
+    each(1, ndp, lambda s: z_sum((dp + s) % ndp, dp).wait_send())
+
+
+def wide_kernel(
     ndp, npool, nx, ny,
     idx_ref, slot_ref, lens_ref, meta_ref, q_ref, c_ref, table_ref, bias_ref,
     att_ref, dq_ref, grad_ref, bgrad_ref,
@@ -207,7 +567,7 @@
     each(1, ndp, lambda s: z_copy((dp + s) % ndp, dp).wait_send())
 
 
-def body(ndp, npool, nx, ny, queries, cotangent, owner, row, table, lengths, bias):
+def wide(ndp, npool, nx, ny, queries, cotangent, owner, row, table, lengths, bias):
     nspans = owner.shape[0]
     width = queries.shape[1]
     span = queries.shape[0] // nspans
@@ -227,7 +587,7 @@
     dma = pltpu.SemaphoreType.DMA
     rows = GROUP * CAP * span
     att, dq, grad, bgrad = pl.pallas_call(
-        functools.partial(kernel, ndp, npool, nx, ny),
+        functools.partial(wide_kernel, ndp, npool, nx, ny),
         out_shape=(
             jax.ShapeDtypeStruct((nspans, span, width), bf),
             jax.ShapeDtypeStruct((nspans, span, width), bf),
@@ -257,13 +617,83 @@
             dma((ndp,)), dma((ndp,)),
         ],
         compiler_params=pltpu.CompilerParams(
-            collective_id=0, has_side_effects=True, vmem_limit_bytes=56 * 1024 * 1024),
+            collective_id=1, has_side_effects=True, vmem_limit_bytes=56 * 1024 * 1024),
     )(
         idx, slot, lengths.reshape(-1), meta,
         queries.reshape(nspans, span, width), cotangent.reshape(nspans, span, width),
         table, bias,
     )
     return att.reshape(queries.shape), dq.reshape(queries.shape), grad, bgrad
+
+
+def lean(ndp, npool, nx, ny, queries, cotangent, owner, row, table, lengths, bias):
+    nspans = owner.shape[0]
+    width = queries.shape[1]
+    span = queries.shape[0] // nspans
+    nsets, keys, _ = table.shape
+    nrow = 2 * nx
+    bf, f32 = jnp.bfloat16, jnp.float32
+    vmem = pl.BlockSpec(memory_space=pltpu.VMEM)
+    smem = pl.BlockSpec(memory_space=pltpu.SMEM)
+    dma = pltpu.SemaphoreType.DMA
+    rows = ny * span
+    att, dq, grad, bgrad, over = pl.pallas_call(
+        functools.partial(lean_kernel, ndp, npool, nx, ny),
+        out_shape=(
+            jax.ShapeDtypeStruct((nspans, span, width), bf),
+            jax.ShapeDtypeStruct((nspans, span, width), bf),
+            jax.ShapeDtypeStruct(table.shape, bf),
+            jax.ShapeDtypeStruct((1, keys), f32),
+            jax.ShapeDtypeStruct((8, 128), f32),
+        ),
+        in_specs=[smem, vmem, vmem, vmem, vmem, vmem, vmem],
+        out_specs=(vmem, vmem, vmem, vmem, vmem),
+        scratch_shapes=[
+            pltpu.VMEM((8, 128), jnp.int32),
+            pltpu.SMEM((8, 128), jnp.int32),
+            pltpu.VMEM((ny, nrow, 128), jnp.int32),
+            pltpu.VMEM((ny, nrow, 128), jnp.int32),
+            pltpu.SMEM((ny, nrow, 128), jnp.int32),
+            pltpu.VMEM((nrow, ny, 128), jnp.int32),
+            pltpu.VMEM((nrow, ny, 128), jnp.int32),
+            pltpu.SMEM((nrow, ny, 128), jnp.int32),
+            pltpu.VMEM((npool, 2, span, width), bf),
+            pltpu.VMEM((2 * npool, 2, span, width), bf),
+            pltpu.VMEM((2 * npool, 2, span, width), bf),
+            pltpu.VMEM((npool + ny * LEAN, 2, span, width), bf),
+            pltpu.VMEM((ny, LEAN, 2, span, width), bf),
+            pltpu.VMEM((ny, LEAN, 2, span, width), bf),
+            pltpu.VMEM((ny, LEAN, 2, span, width), bf),
+            pltpu.VMEM((nrow, ny, 2, span, width), bf),
+            pltpu.VMEM((nrow, ny, 2, span, width), bf),
+            pltpu.VMEM((rows, keys), bf),
+            pltpu.VMEM((rows, keys), bf),
+            pltpu.VMEM((2, rows, nsets * width), bf),
+            pltpu.VMEM((2, keys, nsets * width), f32),
+            pltpu.VMEM((8, keys + 128), f32),
+            pltpu.VMEM((nrow, 8, keys + 128), f32),
+            pltpu.VMEM((ny, 8, keys + 128), f32),
+            pltpu.VMEM((ndp, 8, keys + 128), f32),
+            dma((3,)), dma((ny,)), dma((ny,)), dma((nrow,)), dma((nrow,)),
+            dma((npool,)), dma((npool,)),
+            dma((npool,)), dma((npool,)),
+            dma((ny,)), dma((ny,)), dma((nrow,)), dma((nrow,)),
+            dma((nrow,)), dma((nrow,)), dma((ny,)), dma((ny,)),
+            dma((nrow,)), dma((nrow,)), dma((ny,)), dma((ny,)), dma((ndp,)), dma((ndp,)),
+        ],
+        compiler_params=pltpu.CompilerParams(
+            collective_id=0, has_side_effects=True, vmem_limit_bytes=56 * 1024 * 1024),
+    )(
+        lengths, owner, row.reshape(1, nspans),
+        queries.reshape(nspans, span, width), cotangent.reshape(nspans, span, width),
+        table, bias,
+    )
+    return (att.reshape(queries.shape), dq.reshape(queries.shape), grad, bgrad), over[0, 0] > 0
+
+
+def body(ndp, npool, nx, ny, *args):
+    outs, short = lean(ndp, npool, nx, ny, *args)
+    return lax.cond(short, lambda kept: wide(ndp, npool, nx, ny, *args), lambda kept: kept, outs)
 
 
 def solution(mesh):

time: 250 us -> 181 us (0.72)
  Pallas kernels: 240 us -> 173 us
    pallas_call x1, Pallas kernels: 240 us -> 173 us  [lean(): pl.pallas_call(functools.partial(lean_kernel, ndp, npool, nx, ny), out_sh...]
    unnamed x19 -> x20, local copies, waits for them, and re-layouts: 6.71 us -> 5.18 us
where the time goes in v2:
time: 181 us
  Pallas kernels  173 us (96%)
  local copies, waits for them, and re-layouts  6.37 us (4%)
    pallas_call x1, Pallas kernels, lean(): pl.pallas_call(functools.partial(lean_kernel, ndp, npool, nx, ny), out_sh...  173 us
    unnamed x20, local copies, waits for them, and re-layouts  5.18 us

profile of v2, /device:TPU:1, one launch (start us, length us, event | category | flops | bytes accessed | tf_op | source)
XLA Modules:
  0.0 180.6 jit_solution(2744126879721579002)
XLA Ops:
  0.6 0.0 copy-start.5
  0.6 0.7 copy-done.5
  1.3 0.0 copy-start.7
  1.3 0.7 copy.20.lens_ref
  2.0 0.0 copy-done.7
  2.0 0.0 copy-start.4
  2.0 0.0 copy-start.6
  2.0 0.7 copy.21.own_ref
  2.7 0.0 copy-done.4
  2.7 0.0 copy-done.6
  2.7 0.0 copy-start
  2.7 0.0 copy-start.1
  2.7 0.0 copy-start.2
  2.7 172.9 %shard_map.102 = (bf16[32,64,128]{2,1,0:T(8,128)(2,1)S(1)}, bf16[32,64,128]{2,1,0:T(8,128)(2,1)S(1)}, bf16[8,256,256]{2,1,0:T(8,128)(2,1)S(1)}, f32[1,256]{1,0:T(1,128)S(1)}, f32[8,128]{1,0:T(8,128)}) custom-call(s32[8,2]{1,0:T(8,128)} %copy.20.lens_ref, s32[32,1]{1,0:T(8,128)} %copy.21.own_ref, s32[1,32]{1,0:T(1,128)S(1)} %bitcast.18, ...), custom_call_target="tpu_custom_call" | custom-call | tf_op jit(solution)/shard_map/pallas_call | solution.py:640
  175.6 1.2 slice.3
  177.5 0.0 copy-done
  177.5 0.0 copy-done.1
  177.5 0.0 copy-done.2
  177.5 0.8 copy.35
  178.3 0.8 copy.36
  179.1 1.0 copy.37
  180.1 0.6 copy.38
  (1 shorter events, 0.0 us)
Async XLA Ops:
  0.6 0.7 copy-start.5
  1.3 0.7 copy-start.7
  2.0 0.7 copy-start.4
  2.0 0.7 copy-start.6
  2.7 174.8 %copy-start = (bf16[8,256,256]{2,1,0:T(8,128)(2,1)S(1)}, bf16[8,256,256]{2,1,0:T(8,128)(2,1)}, u32[]{:S(2)}) copy-start(bf16[8,256,256]{2,1,0:T(8,128)(2,1)} %table_ref.1) | copy-start | bytes 3145732
  2.7 174.8 %copy-start.1 = (bf16[2048,128]{1,0:T(8,128)(2,1)S(1)}, bf16[2048,128]{1,0:T(8,128)(2,1)}, u32[]{:S(2)}) copy-start(bf16[2048,128]{1,0:T(8,128)(2,1)} %param.9) | copy-start | bytes 1572868
  2.7 174.8 %copy-start.2 = (bf16[2048,128]{1,0:T(8,128)(2,1)S(1)}, bf16[2048,128]{1,0:T(8,128)(2,1)}, u32[]{:S(2)}) copy-start(bf16[2048,128]{1,0:T(8,128)(2,1)} %param.10) | copy-start | bytes 1572868
